TPU v7x, 256 devices: a whole 4x4x8 slice. The times are simulated.
256 devices in a mesh: dp: 8 (over z), expert: 32 (over x, y, core).
Axes of the slice: x: 4, y: 4, z: 8, core: 2. Of those that a mesh axis runs over, the one named last changes fastest.
Arguments:
- tokens: bfloat16 [32768, 3584], P(('dp', 'expert')), may hold values from -6 to 6
- routes: int32 [32768, 2], P(('dp', 'expert')), may hold values from 0 to 31, all different within a row; in each aligned block of 128 rows (0 to 127, 128 to 255, ...) at most 10 rows name the same one
- scores: bfloat16 [32768, 2], P(('dp', 'expert')), may hold values from 0.099609375 to 1
- out_grad: bfloat16 [32768, 3584], P(('dp', 'expert')), may hold values from -0.8984375 to 0.8984375
- w_up: bfloat16 [32, 1024, 3584], P('expert', 'dp'), may hold values from -0.09375 to 0.09375
- w_down: bfloat16 [32, 1024, 3584], P('expert', 'dp'), may hold values from -0.1875 to 0.1875
Outputs:
- grad_tokens: bfloat16 [32768, 3584], P(('dp', 'expert'))
- grad_scores: bfloat16 [32768, 2], P(('dp', 'expert'))
- grad_up: bfloat16 [32, 1024, 3584], P('expert', 'dp')
- grad_down: bfloat16 [32, 1024, 3584], P('expert', 'dp')
Inputs may be any that keep to these rules, and one draw needn't show every extreme that they name: `routes`: each row names 2 different experts. Among the 128 rows of one device no expert is named more than 10 times, and in every draw some device names some expert exactly 10 times.
All inputs are finite; a program needn't handle non-finite values.
Results may differ from a plain program's by a relative error of at most 0.017.
Values may be sent and summed in bfloat16 or wider, within the bound.
A program may use at most 192 MiB of HBM per device.

v0:
```python
import jax
import jax.numpy as jnp
from jax import lax
from jax.sharding import PartitionSpec as P


def silu_grad(preact):
    sig = jax.nn.sigmoid(preact)
    return sig * (1.0 + preact * (1.0 - sig))


def expert_forward(inputs, up_rows, down_rows):
    preact = jnp.einsum("rd,fd->rf", inputs, up_rows, preferred_element_type=jnp.float32)
    active = jax.nn.silu(preact).astype(jnp.bfloat16)
    output = jnp.dot(active, down_rows, preferred_element_type=jnp.float32)
    return (preact, active, output)


def expert_backward(inputs, grads, slot_scores, up_rows, down_rows):
    preact, active, output = expert_forward(inputs, up_rows, down_rows)
    score_part = jnp.sum(grads.astype(jnp.float32) * output, axis=1)
    weighted = (slot_scores.astype(jnp.float32)[:, None] * grads.astype(jnp.float32)).astype(
        jnp.bfloat16
    )
    hidden_grad = jnp.einsum("rd,fd->rf", weighted, down_rows, preferred_element_type=jnp.float32)
    pre_grad = (hidden_grad * silu_grad(preact)).astype(jnp.bfloat16)
    token_part = jnp.dot(pre_grad, up_rows, preferred_element_type=jnp.float32)
    return (active, weighted, pre_grad, token_part, score_part)


def local(tokens, routes, scores, out_grad, w_up, w_down):
    experts = lax.axis_size("expert")
    tok_count, top_k = routes.shape
    features = tokens.shape[1]
    capacity = 5 * tok_count * top_k // (4 * experts)
    slot_count = experts * capacity
    flat_routes = routes.reshape(tok_count * top_k)
    onehot = (flat_routes[:, None] == jnp.arange(experts, dtype=jnp.int32)[None, :]).astype(
        jnp.int32
    )
    before = jnp.cumsum(onehot, axis=0) - onehot
    order_rank = jnp.sum(before * onehot, axis=1)
    target = flat_routes * capacity + order_rank
    placing = target[:, None] == jnp.arange(slot_count, dtype=jnp.int32)[None, :]
    token_map = jnp.any(placing.reshape(tok_count, top_k, slot_count), axis=1).astype(jnp.bfloat16)
    sent_tokens = jnp.einsum(
        "ts,td->sd", token_map, tokens, preferred_element_type=jnp.float32
    ).astype(jnp.bfloat16)
    sent_grads = jnp.einsum(
        "ts,td->sd", token_map, out_grad, preferred_element_type=jnp.float32
    ).astype(jnp.bfloat16)
    flat_scores = scores.reshape(tok_count * top_k).astype(jnp.float32)
    sent_scores = jnp.sum(jnp.where(placing, flat_scores[:, None], 0.0), axis=0).astype(
        jnp.bfloat16
    )
    recv_tokens, recv_grads, recv_scores = (
        lax.all_to_all(
            sent_tokens.reshape(experts, capacity, features),
            "expert",
            split_axis=0,
            concat_axis=0,
            tiled=True,
        ),
        lax.all_to_all(
            sent_grads.reshape(experts, capacity, features),
            "expert",
            split_axis=0,
            concat_axis=0,
            tiled=True,
        ),
        lax.all_to_all(
            sent_scores.reshape(experts, capacity),
            "expert",
            split_axis=0,
            concat_axis=0,
            tiled=True,
        ),
    )
    recv_tokens = recv_tokens.reshape(slot_count, features)
    recv_grads = recv_grads.reshape(slot_count, features)
    recv_scores = recv_scores.reshape(slot_count)
    full_up, full_down = (
        lax.all_gather(w_up, "dp", axis=1, tiled=True),
        lax.all_gather(w_down, "dp", axis=1, tiled=True),
    )
    active, weighted, pre_grad, token_part, score_part = expert_backward(
        recv_tokens, recv_grads, recv_scores, full_up[0], full_down[0]
    )
    token_grad = token_part.astype(jnp.bfloat16)
    score_grad = score_part.astype(jnp.bfloat16)
    up_term = jnp.einsum("rf,rd->fd", pre_grad, recv_tokens, preferred_element_type=jnp.float32)
    down_term = jnp.einsum("rf,rd->fd", active, weighted, preferred_element_type=jnp.float32)
    summed = lax.psum_scatter(
        jnp.concatenate([up_term, down_term], axis=1).astype(jnp.bfloat16),
        "dp",
        scatter_dimension=0,
        tiled=True,
    ).astype(jnp.float32)
    grad_up = summed[:, :features].astype(jnp.bfloat16)[None]
    grad_down = summed[:, features:].astype(jnp.bfloat16)[None]
    back_tokens, back_scores = (
        lax.all_to_all(
            token_grad.reshape(experts, capacity, features),
            "expert",
            split_axis=0,
            concat_axis=0,
            tiled=True,
        ),
        lax.all_to_all(
            score_grad.reshape(experts, capacity), "expert", split_axis=0, concat_axis=0, tiled=True
        ),
    )
    back_tokens = back_tokens.reshape(slot_count, features)
    back_scores = back_scores.reshape(slot_count).astype(jnp.float32)
    grad_tokens = jnp.einsum(
        "ts,sd->td", token_map, back_tokens, preferred_element_type=jnp.float32
    ).astype(jnp.bfloat16)
    grad_scores = (
        jnp.sum(jnp.where(placing, back_scores[None, :], 0.0), axis=1)
        .reshape(tok_count, top_k)
        .astype(jnp.bfloat16)
    )
    return (grad_tokens, grad_scores, grad_up, grad_down)


def solution(mesh):
    in_specs = (
        P(("dp", "expert"), None),
        P(("dp", "expert"), None),
        P(("dp", "expert"), None),
        P(("dp", "expert"), None),
        P("expert", "dp", None),
        P("expert", "dp", None),
    )
    out_specs = (
        P(("dp", "expert"), None),
        P(("dp", "expert"), None),
        P("expert", "dp", None),
        P("expert", "dp", None),
    )
    return jax.shard_map(local, mesh=mesh, in_specs=in_specs, out_specs=out_specs, check_vma=False)
```

profile of v0, /device:TPU:29, one launch (start us, length us, event | category | flops | bytes accessed | tf_op | source)
XLA Modules:
  0.0 409.7 jit_solution(12770050696548397091)
XLA Ops:
  7.2 0.0 copy-start
  7.2 0.0 copy-start.4
  7.2 0.0 all-gather.5.cloned.1.call-start
  7.2 0.7 all-gather.5.cloned.1.call-update
  7.9 0.0 all-gather.3.cloned.1.call-start
  8.0 0.7 all-gather.3.cloned.1.call-update
  8.7 0.8 copy.37
  9.5 0.1 eq.45
  9.6 0.1 eq.49
  9.8 0.6 reduce-window.6
  10.4 0.2 slice_reduce_fusion
  10.6 0.1 fusion.27
  10.7 0.1 reduce_sum.39
  10.8 0.1 copy.40
  10.9 0.0 copy-done.4
  10.9 0.1 fusion.24
  11.0 0.0 copy-done
  11.0 0.7 convolution_convert_fusion.2
  11.7 2.6 reshape.131
  14.3 7.8 %all-to-all-start.2 = ((bf16[32,10,3584]{2,1,0:T(8,128)(2,1)}), bf16[32,10,3584]{2,1,0:T(8,128)(2,1)}, u32[]{:S(2)}, u32[]{:S(2)}) async-start(bf16[32,10,3584]{2,1,0:T(8,128)(2,1)} %reshape.131), calls=%async_computation.2 | async-start | bytes 7340032 | tf_op jit(solution)/shard_map/all_to_all | solution.py:57
  22.1 0.0 copy-done.3
  22.1 0.7 convolution_convert_fusion.3
  22.9 2.7 reshape.130
  25.5 38.7 %all-to-all-done.2 = bf16[32,10,3584]{2,1,0:T(8,128)(2,1)} async-done(((bf16[32,10,3584]{2,1,0:T(8,128)(2,1)}), bf16[32,10,3584]{2,1,0:T(8,128)(2,1)}, u32[]{:S(2)}, u32[]{:S(2)}) %all-to-all-start.2) | async-done | bytes 2293792 | tf_op jit(solution)/shard_map/all_to_all | solution.py:57
  64.3 10.7 %all-to-all-start.1 = ((bf16[32,10,3584]{2,1,0:T(8,128)(2,1)}), bf16[32,10,3584]{2,1,0:T(8,128)(2,1)}, u32[]{:S(2)}, u32[]{:S(2)}) async-start(bf16[32,10,3584]{2,1,0:T(8,128)(2,1)} %reshape.130), calls=%async_computation.1 | async-start | bytes 7340032 | tf_op jit(solution)/shard_map/all_to_all | solution.py:64
  74.9 3.2 reshape.132
  78.1 39.0 %all-to-all-done.1 = bf16[32,10,3584]{2,1,0:T(8,128)(2,1)} async-done(((bf16[32,10,3584]{2,1,0:T(8,128)(2,1)}), bf16[32,10,3584]{2,1,0:T(8,128)(2,1)}, u32[]{:S(2)}, u32[]{:S(2)}) %all-to-all-start.1) | async-done | bytes 2293792 | tf_op jit(solution)/shard_map/all_to_all | solution.py:64
  117.1 4.9 %reshape.137 = f32[320,3584]{1,0:T(8,128)} reshape(bf16[32,10,3584]{2,1,0:T(8,128)(2,1)} %all-to-all-done.1) | data formatting | bytes 6881280 | tf_op jit(solution)/shard_map/convert_element_type | solution.py:22
  122.0 6.8 %fusion.2 = f32[320,1024]{1,0:T(8,128)} fusion(bf16[320,3584]{1,0:T(8,128)(2,1)S(1)} %reshape.132, bf16[1,1024,3584]{2,1,0:T(8,128)(2,1)} %all-gather.5.cloned.1.call-done), kind=kOutput, calls=%fused_computation.5 | convolution fusion | flops 2348810240 | bytes 10944512 | tf_op jit(solution)/shard_map/rd,fd->rf/dot_general | solution.py:13
  128.8 52.8 %all-gather.3.cloned.1.call-done = bf16[1,1024,3584]{2,1,0:T(8,128)(2,1)} async-done(((bf16[1,128,3584]{2,1,0:T(8,128)(2,1)}), bf16[1,1024,3584]{2,1,0:T(8,128)(2,1)}) %all-gather.3.cloned.1.call-update) | async-done | bytes 7340048 | tf_op jit(solution)/shard_map/all_gather | solution.py:84
  181.5 7.4 %fusion.15 = bf16[320]{0:T(512)(128)(2,1)S(1)} fusion(f32[320,3584]{1,0:T(8,128)} %reshape.137, bf16[1,1024,3584]{2,1,0:T(8,128)(2,1)} %all-gather.3.cloned.1.call-done, f32[320,1024]{1,0:T(8,128)} %fusion.2), kind=kOutput, calls=%fused_computation.19 | convolution fusion | flops 2352742144 | bytes 13238912 | tf_op jit(solution)/shard_map/dot_general | solution.py:15
  189.0 0.7 convert_element_type.152
  189.7 7.7 %all-to-all-start.4 = ((bf16[32,1,10]{2,1,0:T(2,128)(2,1)}), bf16[32,1,10]{2,1,0:T(2,128)(2,1)S(1)}, u32[]{:S(2)}, u32[]{:S(2)}) async-start(bf16[32,1,10]{2,1,0:T(2,128)(2,1)} %convert_element_type.152), calls=%async_computation.4 | async-start | bytes 32768 | tf_op jit(solution)/shard_map/all_to_all | solution.py:109
  197.4 0.0 reduce-scatter.2.cloned.1.call-start
  197.5 0.0 copy-done.5
  197.5 0.1 copy.41
  197.6 0.1 reshape.135
  197.7 3.0 all-to-all-done.4
  200.7 0.1 convert_reduce_fusion
  200.8 0.1 reshape.138
  200.9 0.2 select_reduce_fusion
  201.1 0.1 convert_element_type.151
  201.2 10.7 %all_to_all.27 = bf16[32,1,10]{2,1,0:T(2,128)(2,1)S(1)} all-to-all(bf16[32,1,10]{2,1,0:T(2,128)(2,1)S(1)} %convert_element_type.151), channel_id=1, replica_groups=mesh['dp'=8,'expert'=32] {'expert'}, dimensions={0} | all-to-all | bytes 1280 | tf_op jit(solution)/shard_map/all_to_all | solution.py:71
  211.9 0.1 convert_reduce_fusion.1
  211.9 0.1 reshape.139
  212.0 5.1 %multiply_convert_fusion = bf16[32,10,3584]{2,1,0:T(8,128)(2,1)} fusion(f32[32,10]{1,0:T(8,128)S(1)} %bitcast.55, bf16[32,10,3584]{2,1,0:T(8,128)(2,1)} %all-to-all-done.1), kind=kLoop, calls=%fused_computation.11 | loop fusion | flops 3440640 | bytes 4588800 | tf_op jit(solution)/shard_map/convert_element_type | solution.py:22
  217.1 4.5 %convert_element_type.129 = bf16[320,3584]{1,0:T(8,128)(2,1)} reshape(bf16[32,10,3584]{2,1,0:T(8,128)(2,1)} %multiply_convert_fusion) | data formatting | bytes 4587520 | tf_op jit(solution)/shard_map/convert_element_type | solution.py:22
  221.6 7.0 %convolution_convert_fusion = bf16[1024,3584]{1,0:T(8,128)(2,1)S(1)} fusion(f32[320,3584]{1,0:T(8,128)} %reshape.137, f32[320]{0:T(512)S(1)} %reshape.139, f32[320,1024]{1,0:T(8,128)} %fusion.2), kind=kOutput, calls=%fused_computation.1 | convolution fusion | flops 2356412416 | bytes 13239552 | tf_op jit(solution)/shard_map/rf,rd->fd/dot_general | solution.py:92
  228.6 0.0 copy-done.2
  228.6 5.7 %fusion.21 = bf16[320,1024]{1,0:T(8,128)(2,1)S(1)} fusion(bf16[320,3584]{1,0:T(8,128)(2,1)S(1)} %copy-done.2, bf16[1,1024,3584]{2,1,0:T(8,128)(2,1)} %all-gather.3.cloned.1.call-done, f32[320,1024]{1,0:T(8,128)S(1)} %copy-done.6), kind=kOutput, calls=%fused_computation.21 | convolution fusion | flops 2351759360 | bytes 11599872 | tf_op jit(solution)/shard_map/rd,fd->rf/dot_general | solution.py:25
  234.4 4.3 %convolution_convert_fusion.1 = bf16[1024,3584]{1,0:T(8,128)(2,1)S(1)} fusion(bf16[320,1024]{1,0:T(8,128)(2,1)S(1)} %fusion.21, bf16[320,3584]{1,0:T(8,128)(2,1)S(1)} %reshape.132), kind=kOutput, calls=%fused_computation.2 | convolution fusion | flops 2352480256 | bytes 10289152 | tf_op jit(solution)/shard_map/rf,rd->fd/dot_general | solution.py:91
  238.7 8.8 %pad_maximum_fusion = bf16[1024,7168]{1,0:T(8,128)(2,1)} fusion(bf16[1024,3584]{1,0:T(8,128)(2,1)S(1)} %convolution_convert_fusion, bf16[1024,3584]{1,0:T(8,128)(2,1)S(1)} %convolution_convert_fusion.1), kind=kLoop, calls=%fused_computation | loop fusion | flops 29360128 | bytes 29360128 | tf_op jit(solution)/shard_map/concatenate | solution.py:94
  247.4 0.0 reduce-scatter.2.cloned.1.call-update
  247.4 5.6 %fusion.11 = bf16[320,3584]{1,0:T(8,128)(2,1)S(1)} fusion(bf16[320,1024]{1,0:T(8,128)(2,1)S(1)} %fusion.21, bf16[1,1024,3584]{2,1,0:T(8,128)(2,1)} %all-gather.5.cloned.1.call-done), kind=kOutput, calls=%fused_computation.13 | convolution fusion | flops 2349957120 | bytes 10289152 | tf_op jit(solution)/shard_map/dot_general | solution.py:27
  253.1 2.6 reshape.133
  255.7 8.8 %all-to-all-start.3 = ((bf16[32,10,3584]{2,1,0:T(8,128)(2,1)}), bf16[32,10,3584]{2,1,0:T(8,128)(2,1)}, u32[]{:S(2)}, u32[]{:S(2)}) async-start(bf16[32,10,3584]{2,1,0:T(8,128)(2,1)} %reshape.133), calls=%async_computation.3 | async-start | bytes 7340032 | tf_op jit(solution)/shard_map/all_to_all | solution.py:102
  264.5 0.2 convert_element_type.142
  264.6 0.6 copy.44
  265.2 41.2 %all-to-all-done.3 = bf16[32,10,3584]{2,1,0:T(8,128)(2,1)} async-done(((bf16[32,10,3584]{2,1,0:T(8,128)(2,1)}), bf16[32,10,3584]{2,1,0:T(8,128)(2,1)}, u32[]{:S(2)}, u32[]{:S(2)}) %all-to-all-start.3) | async-done | bytes 2293792 | tf_op jit(solution)/shard_map/all_to_all | solution.py:102
  306.5 3.2 reshape.134
  309.7 0.0 copy-start.1
  309.7 1.6 convolution_convert_fusion.4
  311.3 89.0 %reduce-scatter.2.cloned.1.call-done = bf16[128,7168]{1,0:T(8,128)(2,1)} async-done(((bf16[1024,7168]{1,0:T(8,128)(2,1)}), bf16[128,7168]{1,0:T(8,128)(2,1)}) %reduce-scatter.2.cloned.1.call-update) | async-done | bytes 1835024 | tf_op jit(solution)/shard_map/reduce_scatter | solution.py:93
  400.4 2.8 slice_bitcast_fusion
  (13 shorter events, 0.1 us)
Async XLA Ops:
  7.2 3.8 copy-start
  7.2 3.7 copy-start.4
  7.2 114.8 %all-gather.5.cloned.1.call-start = ((), (), s32[]{:S(2)}) async-start(), calls=%async_computation.7 | async-start | bytes 8257536 | tf_op jit(solution)/shard_map/all_gather | solution.py:83
  7.9 173.6 %all-gather.3.cloned.1.call-start = ((), (), s32[]{:S(2)}) async-start(), calls=%async_computation.6 | async-start | bytes 8257536 | tf_op jit(solution)/shard_map/all_gather | solution.py:84
  14.3 7.8 %copy-start.3 = (bf16[128,3584]{1,0:T(8,128)(2,1)S(1)}, bf16[128,3584]{1,0:T(8,128)(2,1)}, u32[]{:S(2)}) copy-start(bf16[128,3584]{1,0:T(8,128)(2,1)} %param.9) | copy-start | bytes 2752516
  14.3 49.9 %all-to-all-start.2 = ((bf16[32,10,3584]{2,1,0:T(8,128)(2,1)}), bf16[32,10,3584]{2,1,0:T(8,128)(2,1)}, u32[]{:S(2)}, u32[]{:S(2)}) async-start(bf16[32,10,3584]{2,1,0:T(8,128)(2,1)} %reshape.131), calls=%async_computation.2 | async-start | bytes 7340032 | tf_op jit(solution)/shard_map/all_to_all | solution.py:57
  64.3 52.8 %all-to-all-start.1 = ((bf16[32,10,3584]{2,1,0:T(8,128)(2,1)}), bf16[32,10,3584]{2,1,0:T(8,128)(2,1)}, u32[]{:S(2)}, u32[]{:S(2)}) async-start(bf16[32,10,3584]{2,1,0:T(8,128)(2,1)} %reshape.130), calls=%async_computation.1 | async-start | bytes 7340032 | tf_op jit(solution)/shard_map/all_to_all | solution.py:64
  128.8 68.7 %copy-start.5 = (bf16[128,2]{0,1:T(2,128)(2,1)S(1)}, bf16[128,2]{0,1:T(2,128)(2,1)}, u32[]{:S(2)}) copy-start(bf16[128,2]{0,1:T(2,128)(2,1)} %param.8) | copy-start | bytes 1540
  189.7 11.0 %all-to-all-start.4 = ((bf16[32,1,10]{2,1,0:T(2,128)(2,1)}), bf16[32,1,10]{2,1,0:T(2,128)(2,1)S(1)}, u32[]{:S(2)}, u32[]{:S(2)}) async-start(bf16[32,1,10]{2,1,0:T(2,128)(2,1)} %convert_element_type.152), calls=%async_computation.4 | async-start | bytes 32768 | tf_op jit(solution)/shard_map/all_to_all | solution.py:109
  197.4 203.0 %reduce-scatter.2.cloned.1.call-start = ((), (), s32[]{:S(2)}) async-start(), calls=%async_computation.8 | async-start | bytes 16515072 | tf_op jit(solution)/shard_map/reduce_scatter | solution.py:93
  221.6 7.0 %copy-start.2 = (bf16[320,3584]{1,0:T(8,128)(2,1)S(1)}, bf16[320,3584]{1,0:T(8,128)(2,1)}, u32[]{:S(2)}) copy-start(bf16[320,3584]{1,0:T(8,128)(2,1)} %convert_element_type.129) | copy-start | bytes 6881284
  221.6 7.0 %copy-start.6 = (f32[320,1024]{1,0:T(8,128)S(1)}, f32[320,1024]{1,0:T(8,128)}, u32[]{:S(2)}) copy-start(f32[320,1024]{1,0:T(8,128)} %fusion.2) | copy-start | bytes 3932164
  255.7 50.8 %all-to-all-start.3 = ((bf16[32,10,3584]{2,1,0:T(8,128)(2,1)}), bf16[32,10,3584]{2,1,0:T(8,128)(2,1)}, u32[]{:S(2)}, u32[]{:S(2)}) async-start(bf16[32,10,3584]{2,1,0:T(8,128)(2,1)} %reshape.133), calls=%async_computation.3 | async-start | bytes 7340032 | tf_op jit(solution)/shard_map/all_to_all | solution.py:102
  309.7 93.5 %copy-start.1 = (bf16[128,3584]{1,0:T(8,128)(2,1)S(1)}, bf16[128,3584]{1,0:T(8,128)(2,1)}, u32[]{:S(2)}) copy-start(bf16[128,3584]{1,0:T(8,128)(2,1)} %param.6) | copy-start | bytes 2752516
Sparse Core Ops, SparseCore 0:
  9.8 86.9 all-gather.4
  98.6 82.8 all-gather.2
  247.6 152.7 reduce-scatter.1
where the time goes:
time: 412 us; the launch traced here: 410 us
  waiting for transfers between devices  265 us (64%)
  matrix products  39.9 us (10%)
  starting transfers between devices  35 us (8%)
  local copies, waits for them, and re-layouts  30 us (7%)
  other arithmetic  15 us (4%)
  between operations  14 us (3%)
  blocking collectives  10.7 us (3%)
    reduce_scatter x1, waiting for transfers between devices, local(): lax.psum_scatter(jnp.concatenate([up_term, down_term], axis=1).astype(jnp...  89 us
    all_gather x1, waiting for transfers between devices, local(): lax.all_gather(w_down, 'dp', axis=1, tiled=True)  52.8 us
    all_to_all x1, waiting for transfers between devices, local(): lax.all_to_all(token_grad.reshape(experts, capacity, features), 'expert',...  41.2 us
    all_to_all x1, waiting for transfers between devices, local(): lax.all_to_all(sent_grads.reshape(experts, capacity, features), 'expert',...  39 us
    all_to_all x1, waiting for transfers between devices, local(): lax.all_to_all(sent_tokens.reshape(experts, capacity, features), 'expert'...  38.7 us
    all_to_all x1, blocking collectives, local(): lax.all_to_all(sent_scores.reshape(experts, capacity), 'expert', split_ax...  10.7 us
    all_to_all x1, starting transfers between devices, local(): lax.all_to_all(sent_grads.reshape(experts, capacity, features), 'expert',...  10.7 us
    all_to_all x1, starting transfers between devices, local(): lax.all_to_all(token_grad.reshape(experts, capacity, features), 'expert',...  8.77 us
  transfers between devices with their start and end apart: 7, of which 6 were waited for; matrix products, arithmetic and copies ran while one was open for 9% of the time, Pallas kernels for 0%

commit v1 on v0

v1 whole, which is shorter than its diff:
```python
import functools

import jax
import jax.numpy as jnp
from jax import lax
from jax.experimental import pallas as pl
from jax.experimental.pallas import tpu as pltpu
from jax.sharding import PartitionSpec as P

MESH = pl.DeviceIdType.MESH
BF = jnp.bfloat16
F32 = jnp.float32
ROWS = 16
LANES = 128


def dot_nn(a, b):
    return lax.dot_general(a, b, (((1,), (0,)), ((), ())), preferred_element_type=F32)


def dot_nt(a, b):
    return lax.dot_general(a, b, (((1,), (1,)), ((), ())), preferred_element_type=F32)


def kernel(
    n_dp, n_ex, D, FB, T,
    tok_ref, grad_ref, up_ref, down_ref, routes_ref, scores_ref,
    gtok_ref, gscore_ref, gup_ref, gdown_ref,
    tokv, gradv, send, recv, back, wup, wdn, rs, far, du, dut, ht, sacc, pmat,
    loc_sem, ag_s, ag_r, di_s, di_r, re_s, re_r, rs_s, rs_r, far_s, out_sem,
):
    g = lax.axis_index("dp")
    me = lax.axis_index("expert")
    right, left = lax.rem(g + 1, n_dp), lax.rem(g + n_dp - 1, n_dp)
    S = n_ex * ROWS
    H = D // 2

    loads = [
        pltpu.make_async_copy(tok_ref, tokv, loc_sem.at[0]),
        pltpu.make_async_copy(grad_ref, gradv, loc_sem.at[1]),
        pltpu.make_async_copy(up_ref, wup.at[pl.ds(0, FB)], loc_sem.at[2]),
        pltpu.make_async_copy(down_ref, wdn.at[pl.ds(0, FB)], loc_sem.at[3]),
    ]
    for c in loads:
        c.start()

    barrier = pltpu.get_barrier_semaphore()
    for z in (right, left):
        pl.semaphore_signal(barrier, inc=1, device_id=(z, me), device_id_type=MESH)

    def greet(d, _):
        pl.semaphore_signal(
            barrier, inc=1, device_id=(g, lax.rem(me + d, n_ex)), device_id_type=MESH
        )
        return 0

    lax.fori_loop(1, n_ex, greet, 0)
    pl.semaphore_wait(barrier, n_ex + 1)

    def slot(arm, d):
        return 0 if d == 0 else (7 if d == 4 else 2 * d - 1 + arm)

    def ag(arm, d, m):
        buf, own = (wup, up_ref) if m == 0 else (wdn, down_ref)
        src = own if d == 1 else buf.at[pl.ds(slot(arm, d - 1) * FB, FB)]
        return pltpu.make_async_remote_copy(
            src_ref=src,
            dst_ref=buf.at[pl.ds(slot(arm, d) * FB, FB)],
            send_sem=ag_s.at[arm, d - 1, m],
            recv_sem=ag_r.at[arm, d - 1, m],
            device_id=(right if arm == 0 else left, me),
            device_id_type=MESH,
        )

    def ag_has(arm, d, m):
        return d <= 3 or m == arm

    def order(arm):
        return (0, 1) if arm == 0 else (1, 0)

    for i in range(2):
        for arm in range(2):
            ag(arm, 1, order(arm)[i]).start()

    def ag_step(d):
        for i in range(2):
            for arm in range(2):
                m = order(arm)[i]
                if ag_has(arm, d, m):
                    ag(arm, d, m).wait_recv()
                    if d < 4 and ag_has(arm, d + 1, m):
                        ag(arm, d + 1, m).start()

    lane = lax.broadcasted_iota(jnp.int32, (T, LANES), 1)
    rels, onehots = [], []
    for k in range(2):
        rel = routes_ref[:, k : k + 1] - me
        rel = jnp.where(rel < 0, rel + n_ex, rel)
        rels.append(rel)
        onehots.append((lane == rel).astype(F32))
    tri = (
        lax.broadcasted_iota(jnp.int32, (T, T), 1) < lax.broadcasted_iota(jnp.int32, (T, T), 0)
    ).astype(F32)
    before = dot_nn(tri.astype(BF), (onehots[0] + onehots[1]).astype(BF))
    slots = lax.broadcasted_iota(jnp.int32, (T, S), 1)
    pts = []
    for k in range(2):
        rank = jnp.sum(before * onehots[k], axis=1, keepdims=True).astype(jnp.int32)
        place = (slots == rels[k] * ROWS + rank).astype(F32)
        pmat[k] = place.astype(BF)
        pts.append(place.T.astype(BF))
    pt = pts[0] + pts[1]
    cols = D // 7
    loads[0].wait()
    for j in range(7):
        send[:, j * cols : (j + 1) * cols] = dot_nn(pt, tokv[:, j * cols : (j + 1) * cols]).astype(BF)
    loads[1].wait()
    for j in range(7):
        send[:, D + j * cols : D + (j + 1) * cols] = dot_nn(
            pt, gradv[:, j * cols : (j + 1) * cols]
        ).astype(BF)
    sc = [jnp.broadcast_to(scores_ref[:, k : k + 1], (T, LANES)) for k in range(2)]
    send[:, 2 * D :] = (dot_nn(pts[0], sc[0]) + dot_nn(pts[1], sc[1])).astype(BF)
    recv[0:ROWS, :] = send[0:ROWS, :]

    def block(d):
        return pl.ds(pl.multiple_of(d * ROWS, ROWS), ROWS)

    def dispatch(d):
        return pltpu.make_async_remote_copy(
            src_ref=send.at[block(d)],
            dst_ref=recv.at[block(d)],
            send_sem=di_s.at[d],
            recv_sem=di_r.at[d],
            device_id=(g, lax.rem(me + d, n_ex)),
            device_id_type=MESH,
        )

    def giveback(d):
        return pltpu.make_async_remote_copy(
            src_ref=send.at[block(d), pl.ds(0, D + LANES)],
            dst_ref=back.at[block(d)],
            send_sem=re_s.at[d],
            recv_sem=re_r.at[d],
            device_id=(g, lax.rem(me + n_ex - d, n_ex)),
            device_id_type=MESH,
        )

    def each(action):
        def body(d, _):
            action(d)
            return 0

        lax.fori_loop(1, n_ex, body, 0)

    each(lambda d: dispatch(d).start())
    sacc[...] = jnp.zeros_like(sacc)

    def hidden(first, count):
        n = count * FB
        rows = slice(first * FB, first * FB + n)
        c = recv[:, 2 * D :].astype(F32)
        if count == 2:
            c = jnp.concatenate([c, c], axis=1)
        u = dot_nt(recv[:, :D], wup[rows, :])
        s = dot_nt(recv[:, D : 2 * D], wdn[rows, :])
        sig = jax.nn.sigmoid(u)
        h = (u * sig).astype(BF).astype(F32)
        score = h * s
        for i in range(count):
            sacc[...] += score[:, i * FB : (i + 1) * FB]
        dpre = c * s * (sig * (1.0 + u * (1.0 - sig)))
        du[:, rows] = dpre.astype(BF)
        dut[rows, :] = dpre.T.astype(BF)
        ht[rows, :] = (h * c).T.astype(BF)

    ag_step(1)
    ag_step(2)
    ag_step(3)
    each(lambda d: dispatch(d).wait_recv())
    for c in loads[2:]:
        c.wait()
    hidden(0, 1)
    for d in (1, 2, 3):
        hidden(2 * d - 1, 2)
    ag_step(4)
    hidden(7, 1)

    def term(chunk, m, half):
        lhs = dut if m == 0 else ht
        at = (0 if m == 0 else D) + half * H
        return dot_nn(lhs[chunk * FB : (chunk + 1) * FB, :], recv[:, at : at + H])

    def rs_copy(arm, d, m, half):
        cs = pl.ds(half * H, H)
        src = far.at[arm, :, cs] if d == 4 else rs.at[arm, d, m, :, cs]
        return pltpu.make_async_remote_copy(
            src_ref=src,
            dst_ref=rs.at[arm, d - 1, m, :, cs],
            send_sem=far_s.at[arm, half] if d == 4 else rs_s.at[arm, d, m, half],
            recv_sem=rs_r.at[arm, d - 1, m, half],
            device_id=(left if arm == 0 else right, me),
            device_id_type=MESH,
        )

    def rs_piece(arm, d, m, half):
        cs = slice(half * H, (half + 1) * H)
        t = term(slot(arm, d), m, half)
        if d == 4:
            far[arm, :, cs] = t.astype(BF)
        elif d == 3 and m != arm:
            rs[arm, d, m, :, cs] = t.astype(BF)
        else:
            rs_copy(arm, d + 1, m, half).wait_recv()
            rs[arm, d, m, :, cs] = (t + rs[arm, d, m, :, cs].astype(F32)).astype(BF)
        rs_copy(arm, d, m, half).start()

    for half in range(2):
        for arm in range(2):
            rs_piece(arm, 4, arm, half)
    for half in range(2):
        for arm in range(2):
            rs_piece(arm, 3, 1 - arm, half)

    each(lambda d: dispatch(d).wait_send())
    for j in range(7):
        send[:, j * cols : (j + 1) * cols] = dot_nn(
            du[...], wup[:, j * cols : (j + 1) * cols]
        ).astype(BF)
    total = jnp.sum(sacc[...], axis=1, keepdims=True)
    send[:, D : D + LANES] = jnp.broadcast_to(total, (S, LANES)).astype(BF)
    back[0:ROWS, :] = send[0:ROWS, 0 : D + LANES]
    each(lambda d: giveback(d).start())

    for half in range(2):
        for arm in range(2):
            rs_piece(arm, 3, arm, half)
    for d in (2, 1):
        for i in range(2):
            for half in range(2):
                for arm in range(2):
                    rs_piece(arm, d, (1 - arm) if i == 0 else arm, half)

    each(lambda d: giveback(d).wait_recv())
    both = pmat[0] + pmat[1]
    for j in range(7):
        tokv[:, j * cols : (j + 1) * cols] = dot_nn(both, back[:, j * cols : (j + 1) * cols]).astype(BF)
    outs = [pltpu.make_async_copy(tokv, gtok_ref, out_sem.at[0])]
    outs[0].start()
    tails = [dot_nn(pmat[k], back[:, D:]) for k in range(2)]
    gscore_ref[...] = jnp.where(lane == 0, tails[0], tails[1])[:, 0:2].astype(BF)

    t_out = 1
    for half in range(2):
        for m in range(2):
            cs = slice(half * H, (half + 1) * H)
            t = term(0, m, half)
            for arm in range(2):
                rs_copy(arm, 1, m, half).wait_recv()
                t = t + rs[arm, 0, m, :, cs].astype(F32)
            rs[0, 0, m, :, cs] = t.astype(BF)
            ref = gup_ref if m == 0 else gdown_ref
            o = pltpu.make_async_copy(
                rs.at[0, 0, m, :, pl.ds(half * H, H)], ref.at[:, pl.ds(half * H, H)], out_sem.at[t_out]
            )
            o.start()
            outs.append(o)
            t_out += 1

    each(lambda d: giveback(d).wait_send())
    for arm in range(2):
        for d in range(1, 5):
            for m in range(2):
                if ag_has(arm, d, m):
                    ag(arm, d, m).wait_send()
                    for half in range(2):
                        rs_copy(arm, d, m, half).wait_send()
    for o in outs:
        o.wait()


def local(tokens, routes, scores, out_grad, w_up, w_down):
    n_dp, n_ex = lax.axis_size("dp"), lax.axis_size("expert")
    T, D = tokens.shape
    FB = w_up.shape[1]
    S = n_ex * ROWS
    F = n_dp * FB
    any_spec = pl.BlockSpec(memory_space=pl.ANY)
    vmem_spec = pl.BlockSpec(memory_space=pltpu.VMEM)
    dma = pltpu.SemaphoreType.DMA
    gt, gs, gu, gd = pl.pallas_call(
        functools.partial(kernel, n_dp, n_ex, D, FB, T),
        out_shape=[
            jax.ShapeDtypeStruct((T, D), BF),
            jax.ShapeDtypeStruct((T, 2), BF),
            jax.ShapeDtypeStruct((FB, D), BF),
            jax.ShapeDtypeStruct((FB, D), BF),
        ],
        in_specs=[any_spec] * 4 + [vmem_spec] * 2,
        out_specs=[any_spec, vmem_spec, any_spec, any_spec],
        scratch_shapes=[
            pltpu.VMEM((T, D), BF),
            pltpu.VMEM((T, D), BF),
            pltpu.VMEM((S, 2 * D + LANES), BF),
            pltpu.VMEM((S, 2 * D + LANES), BF),
            pltpu.VMEM((S, D + LANES), BF),
            pltpu.VMEM((F, D), BF),
            pltpu.VMEM((F, D), BF),
            pltpu.VMEM((2, 4, 2, FB, D), BF),
            pltpu.VMEM((2, FB, D), BF),
            pltpu.VMEM((S, F), BF),
            pltpu.VMEM((F, S), BF),
            pltpu.VMEM((F, S), BF),
            pltpu.VMEM((S, LANES), F32),
            pltpu.VMEM((2, T, S), BF),
            dma((4,)),
            dma((2, 4, 2)),
            dma((2, 4, 2)),
            dma((n_ex,)),
            dma((n_ex,)),
            dma((n_ex,)),
            dma((n_ex,)),
            dma((2, 4, 2, 2)),
            dma((2, 4, 2, 2)),
            dma((2, 2)),
            dma((5,)),
        ],
        compiler_params=pltpu.CompilerParams(
            collective_id=0, has_side_effects=True, vmem_limit_bytes=62 * 2**20
        ),
    )(tokens, out_grad, w_up[0], w_down[0], routes, scores)
    return gt, gs, gu[None], gd[None]


def solution(mesh):
    rows = P(("dp", "expert"), None)
    weights = P("expert", "dp", None)
    return jax.shard_map(
        local,
        mesh=mesh,
        in_specs=(rows, rows, rows, rows, weights, weights),
        out_specs=(rows, rows, weights, weights),
        check_vma=False,
    )
```

time: 412 us -> 341 us (0.83)
  Pallas kernels: 0 us -> 332 us
  waiting for transfers between devices: 265 us -> 0 us
  matrix products: 39.9 us -> 0 us
  starting transfers between devices: 35 us -> 0 us
  local copies, waits for them, and re-layouts: 30 us -> 8.15 us
  other arithmetic: 15 us -> 0 us
  between operations: 14 us -> 0.65 us
  blocking collectives: 10.7 us -> 0 us
    pallas_call x0 -> x1, Pallas kernels: none -> 332 us  [local(): pl.pallas_call(functools.partial(kernel, n_dp, n_ex, D, FB, T), out_shape...]
    all_to_all x4 -> x0, waiting for transfers between devices: 122 us -> none  [the longest x1 41.2 us: local(): lax.all_to_all(token_grad.reshape(experts, capacity, features), 'expert',...]
    reduce_scatter x1 -> x0, waiting for transfers between devices: 89 us -> none  [local(): lax.psum_scatter(jnp.concatenate([up_term, down_term], axis=1).astype(jnp...]
    all_gather x2 -> x0, waiting for transfers between devices: 52.8 us -> none  [the longest x1 52.8 us: local(): lax.all_gather(w_down, 'dp', axis=1, tiled=True)]
    dot_general x9 -> x0, matrix products: 39.9 us -> none  [the longest x1 7.42 us: expert_forward(): output = jnp.dot(active, down_rows, preferred_element_type=jnp.float32)]
    all_to_all x4 -> x0, starting transfers between devices: 34.9 us -> none  [the longest x1 10.7 us: local(): lax.all_to_all(sent_grads.reshape(experts, capacity, features), 'expert',...]
    reshape x5 -> x0, local copies, waits for them, and re-layouts: 14.3 us -> none  [the longest x1 3.21 us: local(): back_tokens = back_tokens.reshape(slot_count, features)]
    convert_element_type x9 -> x0, local copies, waits for them, and re-layouts: 10.9 us -> none  [the longest x1 4.92 us: expert_backward(): grads.astype(jnp.float32)]
  transfers between devices with their start and end apart: 7 -> 0, of which waited for: 6 -> 0; matrix products, arithmetic and copies ran while one was open for 9% -> 0% of each run, Pallas kernels for 0% -> 0%
where the time goes in v1:
time: 341 us
  Pallas kernels  332 us (97%)
  local copies, waits for them, and re-layouts  8.15 us (2%)
    pallas_call x1, Pallas kernels, local(): pl.pallas_call(functools.partial(kernel, n_dp, n_ex, D, FB, T), out_shape...  332 us
    unnamed x14, local copies, waits for them, and re-layouts  8.15 us

profile of v1, /device:TPU:29, one launch (start us, length us, event | category | flops | bytes accessed | tf_op | source)
XLA Modules:
  0.0 341.2 jit_solution(4237710612834028773)
XLA Ops:
  0.6 0.0 copy-start.3
  0.6 0.6 copy-done.3
  1.3 0.0 copy-start.2
  1.3 0.7 copy.11.scores_ref
  2.0 0.0 copy-done.2
  2.0 0.7 copy.10.routes_ref
  2.8 332.4 %shard_map.93 = (bf16[128,3584]{1,0:T(8,128)(2,1)}, bf16[128,2]{1,0:T(8,128)(2,1)}, bf16[128,3584]{1,0:T(8,128)(2,1)}, bf16[128,3584]{1,0:T(8,128)(2,1)}) custom-call(bf16[128,3584]{1,0:T(8,128)(2,1)} %tok_ref.1, bf16[128,3584]{1,0:T(8,128)(2,1)} %grad_ref.1, bf16[128,3584]{1,0:T(8,128)(2,1)} %bitcast.4, bf16[128,3584]{1,0:T(8,128)(2,1)} %bitcast.5, ...), custom_call_target="tpu_custom_call" | custom-call | tf_op jit(solution)/shard_map/pallas_call | solution.py:291
  335.1 1.4 copy.12
  336.5 0.0 copy-start.1
  336.5 2.2 copy.16
  338.7 0.0 copy-done.1
  338.7 0.0 copy-start
  338.7 0.9 copy.17
  339.6 0.6 copy-done
  340.2 0.9 copy.18
Async XLA Ops:
  0.6 0.7 copy-start.3
  1.3 0.7 copy-start.2
  336.5 2.2 copy-start.1
  338.7 1.5 copy-start

commit v2 on v1

--- a/solution.py
+++ b/solution.py
@@ -22,11 +22,33 @@
     return lax.dot_general(a, b, (((1,), (1,)), ((), ())), preferred_element_type=F32)
 
 
+def negative(d):
+    return ((4 - d // 8) % 4) * 8 + ((4 - (d // 2) % 4) % 4) * 2 + d % 2
+
+
+def send_order():
+    def hops(d):
+        x, y = d // 8, (d // 2) % 4
+        return min(x, 4 - x) + min(y, 4 - y)
+
+    pairs = []
+    for d in sorted(range(1, 32), key=lambda d: -hops(d)):
+        for e in (d, negative(d)):
+            if e not in pairs:
+                pairs.append(e)
+    mixed = []
+    while pairs:
+        mixed.append(pairs.pop(0))
+        if pairs:
+            mixed.append(pairs.pop())
+    return mixed
+
+
 def kernel(
     n_dp, n_ex, D, FB, T,
     tok_ref, grad_ref, up_ref, down_ref, routes_ref, scores_ref,
     gtok_ref, gscore_ref, gup_ref, gdown_ref,
-    tokv, gradv, send, recv, back, wup, wdn, rs, far, du, dut, ht, sacc, pmat,
+    tokv, gradv, send, recv, back, wup, wdn, rs, far, du, dut, ht, sacc, pmat, ptt,
     loc_sem, ag_s, ag_r, di_s, di_r, re_s, re_r, rs_s, rs_r, far_s, out_sem,
 ):
     g = lax.axis_index("dp")
@@ -34,6 +56,12 @@
     right, left = lax.rem(g + 1, n_dp), lax.rem(g + n_dp - 1, n_dp)
     S = n_ex * ROWS
     H = D // 2
+    mx, my, mc = me // 8, (me // 2) % 4, me % 2
+
+    def peer(d, sign):
+        px = (mx + sign * (d // 8) + 4) % 4
+        py = (my + sign * ((d // 2) % 4) + 4) % 4
+        return px * 8 + py * 2 + (mc + d) % 2
 
     loads = [
         pltpu.make_async_copy(tok_ref, tokv, loc_sem.at[0]),
@@ -50,7 +78,7 @@
 
     def greet(d, _):
         pl.semaphore_signal(
-            barrier, inc=1, device_id=(g, lax.rem(me + d, n_ex)), device_id_type=MESH
+            barrier, inc=1, device_id=(g, peer(d, 1)), device_id_type=MESH
         )
         return 0
 
@@ -91,25 +119,30 @@
                     if d < 4 and ag_has(arm, d + 1, m):
                         ag(arm, d + 1, m).start()
 
-    lane = lax.broadcasted_iota(jnp.int32, (T, LANES), 1)
+    expert = lax.broadcasted_iota(jnp.int32, (n_ex, T), 0)
     rels, onehots = [], []
     for k in range(2):
-        rel = routes_ref[:, k : k + 1] - me
-        rel = jnp.where(rel < 0, rel + n_ex, rel)
+        to = routes_ref[k : k + 1, :]
+        rx = ((to >> 3) - mx + 4) & 3
+        ry = (((to >> 1) & 3) - my + 4) & 3
+        rel = rx * 8 + ry * 2 + (((to & 1) + mc) & 1)
         rels.append(rel)
-        onehots.append((lane == rel).astype(F32))
+        onehots.append((expert == rel).astype(F32))
     tri = (
-        lax.broadcasted_iota(jnp.int32, (T, T), 1) < lax.broadcasted_iota(jnp.int32, (T, T), 0)
+        lax.broadcasted_iota(jnp.int32, (T, T), 0) < lax.broadcasted_iota(jnp.int32, (T, T), 1)
     ).astype(F32)
-    before = dot_nn(tri.astype(BF), (onehots[0] + onehots[1]).astype(BF))
-    slots = lax.broadcasted_iota(jnp.int32, (T, S), 1)
-    pts = []
+    before = dot_nn((onehots[0] + onehots[1]).astype(BF), tri.astype(BF))
+    slots = lax.broadcasted_iota(jnp.int32, (S, T), 0)
+    score = jnp.zeros((S, 1), F32)
+    pt = jnp.zeros((S, T), F32)
     for k in range(2):
-        rank = jnp.sum(before * onehots[k], axis=1, keepdims=True).astype(jnp.int32)
+        rank = jnp.sum(before * onehots[k], axis=0, keepdims=True).astype(jnp.int32)
         place = (slots == rels[k] * ROWS + rank).astype(F32)
         pmat[k] = place.astype(BF)
-        pts.append(place.T.astype(BF))
-    pt = pts[0] + pts[1]
+        score += jnp.sum(place * scores_ref[k : k + 1, :].astype(F32), axis=1, keepdims=True)
+        pt += place
+    ptt[...] = pt.T.astype(BF)
+    pt = pt.astype(BF)
     cols = D // 7
     loads[0].wait()
     for j in range(7):
@@ -119,8 +152,7 @@
         send[:, D + j * cols : D + (j + 1) * cols] = dot_nn(
             pt, gradv[:, j * cols : (j + 1) * cols]
         ).astype(BF)
-    sc = [jnp.broadcast_to(scores_ref[:, k : k + 1], (T, LANES)) for k in range(2)]
-    send[:, 2 * D :] = (dot_nn(pts[0], sc[0]) + dot_nn(pts[1], sc[1])).astype(BF)
+    send[:, 2 * D :] = jnp.broadcast_to(score, (S, LANES)).astype(BF)
     recv[0:ROWS, :] = send[0:ROWS, :]
 
     def block(d):
@@ -132,7 +164,7 @@
             dst_ref=recv.at[block(d)],
             send_sem=di_s.at[d],
             recv_sem=di_r.at[d],
-            device_id=(g, lax.rem(me + d, n_ex)),
+            device_id=(g, peer(d, 1)),
             device_id_type=MESH,
         )
 
@@ -142,7 +174,7 @@
             dst_ref=back.at[block(d)],
             send_sem=re_s.at[d],
             recv_sem=re_r.at[d],
-            device_id=(g, lax.rem(me + n_ex - d, n_ex)),
+            device_id=(g, peer(d, -1)),
             device_id_type=MESH,
         )
 
@@ -153,7 +185,8 @@
 
         lax.fori_loop(1, n_ex, body, 0)
 
-    each(lambda d: dispatch(d).start())
+    for d in send_order():
+        dispatch(jnp.where(mc == 0, d, negative(d))).start()
     sacc[...] = jnp.zeros_like(sacc)
 
     def hidden(first, count):
@@ -230,7 +263,8 @@
     total = jnp.sum(sacc[...], axis=1, keepdims=True)
     send[:, D : D + LANES] = jnp.broadcast_to(total, (S, LANES)).astype(BF)
     back[0:ROWS, :] = send[0:ROWS, 0 : D + LANES]
-    each(lambda d: giveback(d).start())
+    for d in send_order():
+        giveback(jnp.where(mc == 0, d, negative(d))).start()
 
     for half in range(2):
         for arm in range(2):
@@ -242,13 +276,13 @@
                     rs_piece(arm, d, (1 - arm) if i == 0 else arm, half)
 
     each(lambda d: giveback(d).wait_recv())
-    both = pmat[0] + pmat[1]
     for j in range(7):
-        tokv[:, j * cols : (j + 1) * cols] = dot_nn(both, back[:, j * cols : (j + 1) * cols]).astype(BF)
+        tokv[:, j * cols : (j + 1) * cols] = dot_nn(ptt[...], back[:, j * cols : (j + 1) * cols]).astype(BF)
     outs = [pltpu.make_async_copy(tokv, gtok_ref, out_sem.at[0])]
     outs[0].start()
-    tails = [dot_nn(pmat[k], back[:, D:]) for k in range(2)]
-    gscore_ref[...] = jnp.where(lane == 0, tails[0], tails[1])[:, 0:2].astype(BF)
+    given = back[:, D:].astype(F32)
+    for k in range(2):
+        gscore_ref[k : k + 1, :] = jnp.sum(pmat[k].astype(F32) * given, axis=0, keepdims=True).astype(BF)
 
     t_out = 1
     for half in range(2):
@@ -292,7 +326,7 @@
         functools.partial(kernel, n_dp, n_ex, D, FB, T),
         out_shape=[
             jax.ShapeDtypeStruct((T, D), BF),
-            jax.ShapeDtypeStruct((T, 2), BF),
+            jax.ShapeDtypeStruct((2, T), BF),
             jax.ShapeDtypeStruct((FB, D), BF),
             jax.ShapeDtypeStruct((FB, D), BF),
         ],
@@ -312,7 +346,8 @@
             pltpu.VMEM((F, S), BF),
             pltpu.VMEM((F, S), BF),
             pltpu.VMEM((S, LANES), F32),
-            pltpu.VMEM((2, T, S), BF),
+            pltpu.VMEM((2, S, T), BF),
+            pltpu.VMEM((T, S), BF),
             dma((4,)),
             dma((2, 4, 2)),
             dma((2, 4, 2)),
@@ -328,8 +363,8 @@
         compiler_params=pltpu.CompilerParams(
             collective_id=0, has_side_effects=True, vmem_limit_bytes=62 * 2**20
         ),
-    )(tokens, out_grad, w_up[0], w_down[0], routes, scores)
-    return gt, gs, gu[None], gd[None]
+    )(tokens, out_grad, w_up[0], w_down[0], routes.T, scores.T)
+    return gt, gs.T, gu[None], gd[None]
 
 
 def solution(mesh):

time: 341 us -> 303 us (0.89); the launches traced: 341 us -> 299 us
  Pallas kernels: 332 us -> 293 us
    pallas_call x1, Pallas kernels: 332 us -> 293 us  [local(): pl.pallas_call(functools.partial(kernel, n_dp, n_ex, D, FB, T), out_shape...]
    unnamed x14 -> x10, local copies, waits for them, and re-layouts: 8.15 us -> 5.19 us
where the time goes in v2:
time: 303 us; the launch traced here: 299 us
  Pallas kernels  293 us (97%)
  local copies, waits for them, and re-layouts  5.19 us (2%)
    pallas_call x1, Pallas kernels, local(): pl.pallas_call(functools.partial(kernel, n_dp, n_ex, D, FB, T), out_shape...  293 us

profile of v2, /device:TPU:29, one launch (start us, length us, event | category | flops | bytes accessed | tf_op | source)
XLA Modules:
  0.0 298.7 jit_solution(6884582990945525891)
XLA Ops:
  0.6 292.8 %shard_map.93 = (bf16[128,3584]{1,0:T(8,128)(2,1)}, bf16[2,128]{1,0:T(2,128)(2,1)}, bf16[128,3584]{1,0:T(8,128)(2,1)}, bf16[128,3584]{1,0:T(8,128)(2,1)}) custom-call(bf16[128,3584]{1,0:T(8,128)(2,1)} %tok_ref.1, bf16[128,3584]{1,0:T(8,128)(2,1)} %grad_ref.1, bf16[128,3584]{1,0:T(8,128)(2,1)} %bitcast.9, bf16[128,3584]{1,0:T(8,128)(2,1)} %bitcast.10, ...), custom_call_target="tpu_custom_call" | custom-call | tf_op jit(solution)/shard_map/pallas_call | solution.py:325
  293.5 0.0 copy-start.2
  293.5 0.0 copy-start.1
  293.5 2.2 copy.14
  295.7 0.0 copy-done.2
  295.7 0.5 copy.15
  296.2 0.0 copy-done.1
  296.2 0.0 copy-start
  296.2 0.9 copy.16
  297.2 0.6 copy-done
  297.8 0.9 copy.17
Async XLA Ops:
  293.5 2.3 copy-start.2
  293.5 2.8 copy-start.1
  296.2 1.5 copy-start

commit v3 on v2

--- a/solution.py
+++ b/solution.py
@@ -47,7 +47,7 @@
 def kernel(
     n_dp, n_ex, D, FB, T,
     tok_ref, grad_ref, up_ref, down_ref, routes_ref, scores_ref,
-    gtok_ref, gscore_ref, gup_ref, gdown_ref,
+    gtok_ref, gscore_ref, near_ref, late_ref,
     tokv, gradv, send, recv, back, wup, wdn, rs, far, du, dut, ht, sacc, pmat, ptt,
     loc_sem, ag_s, ag_r, di_s, di_r, re_s, re_r, rs_s, rs_r, far_s, out_sem,
 ):
@@ -209,15 +209,14 @@
 
     ag_step(1)
     ag_step(2)
-    ag_step(3)
     each(lambda d: dispatch(d).wait_recv())
     for c in loads[2:]:
         c.wait()
     hidden(0, 1)
-    for d in (1, 2, 3):
-        hidden(2 * d - 1, 2)
-    ag_step(4)
-    hidden(7, 1)
+    hidden(1, 2)
+    hidden(3, 2)
+    ag_step(3)
+    hidden(5, 2)
 
     def term(chunk, m, half):
         lhs = dut if m == 0 else ht
@@ -229,7 +228,7 @@
         src = far.at[arm, :, cs] if d == 4 else rs.at[arm, d, m, :, cs]
         return pltpu.make_async_remote_copy(
             src_ref=src,
-            dst_ref=rs.at[arm, d - 1, m, :, cs],
+            dst_ref=late_ref.at[m, :, cs] if d == 1 and m == arm else rs.at[arm, d - 1, m, :, cs],
             send_sem=far_s.at[arm, half] if d == 4 else rs_s.at[arm, d, m, half],
             recv_sem=rs_r.at[arm, d - 1, m, half],
             device_id=(left if arm == 0 else right, me),
@@ -250,10 +249,12 @@
 
     for half in range(2):
         for arm in range(2):
-            rs_piece(arm, 4, arm, half)
+            rs_piece(arm, 3, 1 - arm, half)
+    ag_step(4)
+    hidden(7, 1)
     for half in range(2):
         for arm in range(2):
-            rs_piece(arm, 3, 1 - arm, half)
+            rs_piece(arm, 4, arm, half)
 
     each(lambda d: dispatch(d).wait_send())
     for j in range(7):
@@ -284,23 +285,14 @@
     for k in range(2):
         gscore_ref[k : k + 1, :] = jnp.sum(pmat[k].astype(F32) * given, axis=0, keepdims=True).astype(BF)
 
-    t_out = 1
-    for half in range(2):
-        for m in range(2):
+    for m in range(2):
+        for half in range(2):
             cs = slice(half * H, (half + 1) * H)
             t = term(0, m, half)
-            for arm in range(2):
-                rs_copy(arm, 1, m, half).wait_recv()
-                t = t + rs[arm, 0, m, :, cs].astype(F32)
-            rs[0, 0, m, :, cs] = t.astype(BF)
-            ref = gup_ref if m == 0 else gdown_ref
-            o = pltpu.make_async_copy(
-                rs.at[0, 0, m, :, pl.ds(half * H, H)], ref.at[:, pl.ds(half * H, H)], out_sem.at[t_out]
-            )
-            o.start()
-            outs.append(o)
-            t_out += 1
-
+            rs_copy(1 - m, 1, m, half).wait_recv()
+            rs[1 - m, 0, m, :, cs] = (t + rs[1 - m, 0, m, :, cs].astype(F32)).astype(BF)
+        outs.append(pltpu.make_async_copy(rs.at[1 - m, 0, m], near_ref.at[m], out_sem.at[1 + m]))
+        outs[-1].start()
     each(lambda d: giveback(d).wait_send())
     for arm in range(2):
         for d in range(1, 5):
@@ -311,6 +303,9 @@
                         rs_copy(arm, d, m, half).wait_send()
     for o in outs:
         o.wait()
+    for half in range(2):
+        for m in range(2):
+            rs_copy(m, 1, m, half).wait_recv()
 
 
 def local(tokens, routes, scores, out_grad, w_up, w_down):
@@ -322,13 +317,13 @@
     any_spec = pl.BlockSpec(memory_space=pl.ANY)
     vmem_spec = pl.BlockSpec(memory_space=pltpu.VMEM)
     dma = pltpu.SemaphoreType.DMA
-    gt, gs, gu, gd = pl.pallas_call(
+    gt, gs, near, late = pl.pallas_call(
         functools.partial(kernel, n_dp, n_ex, D, FB, T),
         out_shape=[
             jax.ShapeDtypeStruct((T, D), BF),
             jax.ShapeDtypeStruct((2, T), BF),
-            jax.ShapeDtypeStruct((FB, D), BF),
-            jax.ShapeDtypeStruct((FB, D), BF),
+            jax.ShapeDtypeStruct((2, FB, D), BF),
+            jax.ShapeDtypeStruct((2, FB, D), BF),
         ],
         in_specs=[any_spec] * 4 + [vmem_spec] * 2,
         out_specs=[any_spec, vmem_spec, any_spec, any_spec],
@@ -364,6 +359,7 @@
             collective_id=0, has_side_effects=True, vmem_limit_bytes=62 * 2**20
         ),
     )(tokens, out_grad, w_up[0], w_down[0], routes.T, scores.T)
+    gu, gd = ((near[m].astype(F32) + late[m].astype(F32)).astype(BF) for m in range(2))
     return gt, gs.T, gu[None], gd[None]
 
 

time: 303 us -> 299 us (0.987)
  Pallas kernels: 293 us -> 288 us
  local copies, waits for them, and re-layouts: 5.19 us -> 1.44 us
  other arithmetic: 0 us -> 3.74 us
    pallas_call x1, Pallas kernels: 293 us -> 288 us  [local(): pl.pallas_call(functools.partial(kernel, n_dp, n_ex, D, FB, T), out_shape...]
    unnamed x10 -> x6, local copies, waits for them, and re-layouts: 5.19 us -> 1.44 us
    convert_element_type x0 -> x1, other arithmetic: none -> 3.74 us  [local(): (near[m].astype(F32) + late[m].astype(F32)).astype(BF)]
where the time goes in v3:
time: 299 us; the launch traced here: 294 us
  Pallas kernels  288 us (96%)
  other arithmetic  3.74 us (1%)
    pallas_call x1, Pallas kernels, local(): pl.pallas_call(functools.partial(kernel, n_dp, n_ex, D, FB, T), out_shape...  288 us

profile of v3, /device:TPU:29, one launch (start us, length us, event | category | flops | bytes accessed | tf_op | source)
XLA Modules:
  0.0 294.1 jit_solution(13491048771294285455)
XLA Ops:
  0.6 288.3 %shard_map.93 = (bf16[128,3584]{1,0:T(8,128)(2,1)}, bf16[2,128]{1,0:T(2,128)(2,1)}, bf16[2,128,3584]{2,1,0:T(8,128)(2,1)}, bf16[2,128,3584]{2,1,0:T(8,128)(2,1)}) custom-call(bf16[128,3584]{1,0:T(8,128)(2,1)} %tok_ref.1, bf16[128,3584]{1,0:T(8,128)(2,1)} %grad_ref.1, bf16[128,3584]{1,0:T(8,128)(2,1)} %bitcast.5, bf16[128,3584]{1,0:T(8,128)(2,1)} %bitcast.6, ...), custom_call_target="tpu_custom_call" | custom-call | tf_op jit(solution)/shard_map/pallas_call | solution.py:320
  288.9 0.0 copy-start
  288.9 3.7 %add_convert_fusion = (bf16[1,128,3584]{2,1,0:T(8,128)(2,1)}, bf16[1,128,3584]{2,1,0:T(8,128)(2,1)}) fusion(bf16[2,128,3584]{2,1,0:T(8,128)(2,1)} %get-tuple-element.11, bf16[2,128,3584]{2,1,0:T(8,128)(2,1)} %get-tuple-element.10), kind=kLoop, calls=%fused_computation | loop fusion | flops 3670016 | bytes 5505024 | tf_op jit(solution)/shard_map/convert_element_type | solution.py:362
  292.6 0.0 copy-start.1
  292.6 0.0 copy-done
  292.7 0.9 copy.12
  293.6 0.0 copy-done.1
  293.6 0.5 copy.13
Async XLA Ops:
  288.9 3.8 %copy-start = (bf16[128,3584]{1,0:T(8,128)(2,1)S(1)}, bf16[128,3584]{1,0:T(8,128)(2,1)}, u32[]{:S(2)}) copy-start(bf16[128,3584]{1,0:T(8,128)(2,1)} %get-tuple-element.18) | copy-start | bytes 2752516
  292.6 0.9 copy-start.1

commit v4 on v3

--- a/solution.py
+++ b/solution.py
@@ -47,7 +47,7 @@
 def kernel(
     n_dp, n_ex, D, FB, T,
     tok_ref, grad_ref, up_ref, down_ref, routes_ref, scores_ref,
-    gtok_ref, gscore_ref, near_ref, late_ref,
+    gtok_ref, gscore_ref, near_up, near_down, late_up, late_down,
     tokv, gradv, send, recv, back, wup, wdn, rs, far, du, dut, ht, sacc, pmat, ptt,
     loc_sem, ag_s, ag_r, di_s, di_r, re_s, re_r, rs_s, rs_r, far_s, out_sem,
 ):
@@ -228,7 +228,7 @@
         src = far.at[arm, :, cs] if d == 4 else rs.at[arm, d, m, :, cs]
         return pltpu.make_async_remote_copy(
             src_ref=src,
-            dst_ref=late_ref.at[m, :, cs] if d == 1 and m == arm else rs.at[arm, d - 1, m, :, cs],
+            dst_ref=(late_up, late_down)[m].at[:, cs] if d == 1 and m == arm else rs.at[arm, d - 1, m, :, cs],
             send_sem=far_s.at[arm, half] if d == 4 else rs_s.at[arm, d, m, half],
             recv_sem=rs_r.at[arm, d - 1, m, half],
             device_id=(left if arm == 0 else right, me),
@@ -291,7 +291,7 @@
             t = term(0, m, half)
             rs_copy(1 - m, 1, m, half).wait_recv()
             rs[1 - m, 0, m, :, cs] = (t + rs[1 - m, 0, m, :, cs].astype(F32)).astype(BF)
-        outs.append(pltpu.make_async_copy(rs.at[1 - m, 0, m], near_ref.at[m], out_sem.at[1 + m]))
+        outs.append(pltpu.make_async_copy(rs.at[1 - m, 0, m], (near_up, near_down)[m], out_sem.at[1 + m]))
         outs[-1].start()
     each(lambda d: giveback(d).wait_send())
     for arm in range(2):
@@ -317,16 +317,18 @@
     any_spec = pl.BlockSpec(memory_space=pl.ANY)
     vmem_spec = pl.BlockSpec(memory_space=pltpu.VMEM)
     dma = pltpu.SemaphoreType.DMA
-    gt, gs, near, late = pl.pallas_call(
+    gt, gs, *sums = pl.pallas_call(
         functools.partial(kernel, n_dp, n_ex, D, FB, T),
         out_shape=[
             jax.ShapeDtypeStruct((T, D), BF),
             jax.ShapeDtypeStruct((2, T), BF),
-            jax.ShapeDtypeStruct((2, FB, D), BF),
-            jax.ShapeDtypeStruct((2, FB, D), BF),
+            jax.ShapeDtypeStruct((FB, D), BF),
+            jax.ShapeDtypeStruct((FB, D), BF),
+            jax.ShapeDtypeStruct((FB, D), BF),
+            jax.ShapeDtypeStruct((FB, D), BF),
         ],
         in_specs=[any_spec] * 4 + [vmem_spec] * 2,
-        out_specs=[any_spec, vmem_spec, any_spec, any_spec],
+        out_specs=[any_spec, vmem_spec] + [any_spec] * 4,
         scratch_shapes=[
             pltpu.VMEM((T, D), BF),
             pltpu.VMEM((T, D), BF),
@@ -359,7 +361,7 @@
             collective_id=0, has_side_effects=True, vmem_limit_bytes=62 * 2**20
         ),
     )(tokens, out_grad, w_up[0], w_down[0], routes.T, scores.T)
-    gu, gd = ((near[m].astype(F32) + late[m].astype(F32)).astype(BF) for m in range(2))
+    gu, gd = ((sums[m].astype(F32) + sums[2 + m].astype(F32)).astype(BF) for m in range(2))
     return gt, gs.T, gu[None], gd[None]
 
 

time: 299 us -> 299 us (level)
    broadcast_in_dim x0 -> x1, other arithmetic: none -> 3.74 us  [local(): return (gt, gs.T, gu[None], gd[None])]
    convert_element_type x1 -> x0, other arithmetic: 3.74 us -> none  [local(): (near[m].astype(F32) + late[m].astype(F32)).astype(BF)]
where the time goes in v4:
time: 299 us; the launch traced here: 294 us
  Pallas kernels  288 us (96%)
  other arithmetic  3.74 us (1%)
    pallas_call x1, Pallas kernels, local(): pl.pallas_call(functools.partial(kernel, n_dp, n_ex, D, FB, T), out_shape...  288 us

profile of v4, /device:TPU:29, one launch (start us, length us, event | category | flops | bytes accessed | tf_op | source)
XLA Modules:
  0.0 294.1 jit_solution(12690989297791590427)
XLA Ops:
  0.6 288.3 %shard_map.93 = (bf16[128,3584]{1,0:T(8,128)(2,1)}, bf16[2,128]{1,0:T(2,128)(2,1)}, bf16[128,3584]{1,0:T(8,128)(2,1)}, bf16[128,3584]{1,0:T(8,128)(2,1)}, bf16[1...) custom-call(bf16[128,3584]{1,0:T(8,128)(2,1)} %tok_ref.1, bf16[128,3584]{1,0:T(8,128)(2,1)} %grad_ref.1, ...), custom_call_target="tpu_custom_call" | custom-call | tf_op jit(solution)/shard_map/pallas_call | solution.py:320
  288.9 0.0 copy-start
  288.9 3.7 %fusion = (bf16[1,128,3584]{2,1,0:T(8,128)(2,1)}, bf16[1,128,3584]{2,1,0:T(8,128)(2,1)}) fusion(bf16[128,3584]{1,0:T(8,128)(2,1)} %get-tuple-element.13, bf16[128,3584]{1,0:T(8,128)(2,1)} %get-tuple-element.12, bf16[128,3584]{1,0:T(8,128)(2,1)} %get-tuple-element.15, bf16[128,3584]{1,0:T(8,128)(2,1)} %get-tuple-element.14), kind=kLoop, calls=%fused_computation.2 | loop fusion | flops 3670016 | bytes 5505024 | tf_op jit(solution)/shard_map/broadcast_in_dim | solution.py:365
  292.6 0.0 copy-done
  292.7 0.0 copy-start.1
  292.7 0.9 copy.12
  293.6 0.0 copy-done.1
  293.6 0.5 copy.13
Async XLA Ops:
  288.9 3.8 %copy-start = (bf16[128,3584]{1,0:T(8,128)(2,1)S(1)}, bf16[128,3584]{1,0:T(8,128)(2,1)}, u32[]{:S(2)}) copy-start(bf16[128,3584]{1,0:T(8,128)(2,1)} %get-tuple-element.22) | copy-start | bytes 2752516
  292.7 0.9 copy-start.1
